TPU v7x, 256 devices: a whole 4x4x8 slice. The times are simulated.
256 devices in a mesh: pole: 8 (over z), snode: 32 (over y, x, core).
Axes of the slice: x: 4, y: 4, z: 8, core: 2. Of those that a mesh axis runs over, the one named last changes fastest.
Arguments:
- pole_weight: float32 [8, 2], P('pole'), may hold values from -1 to 1
- root_factor: float32 [8, 2, 1024, 1024], P('pole', None, 'snode'), may hold values from -3 to 3, as said below
- leaf_factor: float32 [8, 64, 2, 512, 512], P('pole', 'snode'), may hold values from -3 to 3, as said below
- leaf_upper: float32 [8, 64, 2, 512, 512], P('pole', 'snode'), may hold values from -0.25 to 0.25
- leaf_lower: float32 [8, 64, 2, 512, 512], P('pole', 'snode'), may hold values from -0.25 to 0.25
- face_tiles: int32 [64, 2], P('snode'), may hold values from 0 to 3, all different within a row
Outputs:
- root_density: float32 [1024], P('snode')
- leaf_density: float32 [64, 512], P('snode')
- face_density: float32 [64, 512, 512], P('snode')
Inputs may be any that keep to these rules, and one draw needn't show every extreme that they name: `face_tiles`: each row names 2 different root tiles; every root tile is named by some row. `root_factor`: diagonal tiles hold inverted pivot blocks, the other tiles the unit triangular factors' tiles. `leaf_factor`: laid out as root_factor, with 2 tiles.
All inputs are finite; a program needn't handle non-finite values.
Results may differ from a plain program's by a relative error of at most 0.0003.
Values sent between devices are 32-bit elements; how exact they have to be, the bound alone decides.
A program may use at most 128 MiB of HBM per device.

v0:
```python
import functools

import jax
import jax.numpy as jnp
from jax import lax
from jax.experimental import pallas as pl
from jax.experimental.pallas import tpu as pltpu
from jax.sharding import PartitionSpec as P

NR = 4
X = 4
Y = 4
Z = 8
F32 = jnp.float32
BF16 = jnp.bfloat16


def split(value):
    high = value.astype(BF16)
    return high, (value - high.astype(F32)).astype(BF16)


def as_left(rh, rl, ih, il):
    high = jnp.concatenate([jnp.concatenate([rh, -ih], 1), jnp.concatenate([ih, rh], 1)], 0)
    low = jnp.concatenate([jnp.concatenate([rl, -il], 1), jnp.concatenate([il, rl], 1)], 0)
    return jnp.concatenate([high, high, low], 1)


def as_right(rh, rl, ih, il):
    return jnp.concatenate([rh, ih, rl, il, rh, ih], 0)


def product(left, right):
    return jnp.dot(left, right, preferred_element_type=F32)


def fold_rows(value):
    rows, cols = value.shape
    return jnp.sum(value.reshape(rows // 8, 8, cols), axis=0)


def kernel(
    T,
    w_ref, faces_ref, root_hbm, lf_hbm, lu_hbm, ll_hbm,
    face_out, leaf_out, root_out,
    root_all, fh, fl, gh, gl, lf, lu, lut, ll, lh, lo, contrib, rs_buf, leaf_acc, small,
    in_sem, p1_s, p1_r, p2_s, p2_r, sib_s, sib_r, rs_s, rs_r, ag_s, ag_r, sm_s, sm_r,
):
    z = lax.axis_index("pole")
    s = lax.axis_index("snode")
    core = s % 2
    x = (s // 2) % X
    y = s // (2 * X)
    band = root_hbm.shape[1]
    half = band // 2
    sub = T // 4

    def at_xy(yy, xx, cc):
        return {"snode": (yy * X + xx) * 2 + cc}

    xp, xm, x2 = (x + 1) % X, (x + X - 1) % X, (x + 2) % X
    yp, ym, y2 = (y + 1) % Y, (y + Y - 1) % Y, (y + 2) % Y
    zp, zm = (z + 1) % Z, (z + Z - 1) % Z
    east, west = at_xy(y, xp, core), at_xy(y, xm, core)
    north, south = at_xy(yp, x, core), at_xy(ym, x, core)
    mate = at_xy(y, x, 1 - core)
    above, below = {"pole": zp}, {"pole": zm}

    def remote(src, dst, send, recv, to):
        return pltpu.make_async_remote_copy(
            src_ref=src, dst_ref=dst, send_sem=send, recv_sem=recv,
            device_id=to, device_id_type=pl.DeviceIdType.MESH,
        )

    sent = []

    def push(src, dst, send, recv, to):
        copy = remote(src, dst, send, recv, to)
        copy.start()
        sent.append(copy)

    def arrived(dst, send, recv, to):
        remote(dst, dst, send, recv, to).wait_recv()

    barrier = pltpu.get_barrier_semaphore()
    for to in (east, west, north, south, mate, above, below):
        pl.semaphore_signal(barrier, inc=1, device_id=to, device_id_type=pl.DeviceIdType.MESH)

    loads = [
        pltpu.make_async_copy(root_hbm, root_all.at[:, y, x, core], in_sem.at[0]),
        pltpu.make_async_copy(lf_hbm, lf, in_sem.at[1]),
        pltpu.make_async_copy(lu_hbm, lu, in_sem.at[2]),
        pltpu.make_async_copy(ll_hbm, ll, in_sem.at[3]),
    ]
    loads[0].start()
    pl.semaphore_wait(barrier, 7)

    for part, plus, minus in ((0, east, west), (1, north, south)):
        for number, to in ((0, plus), (1, minus)):
            push(root_hbm.at[part], root_all.at[part, y, x, core],
                 p1_s.at[part, number], p1_r.at[part, number], to)
    for load in loads[1:]:
        load.start()
    for part, plus, minus, near in (
        (0, east, west, (root_all.at[0, y, xm, core], root_all.at[0, y, xp, core])),
        (1, north, south, (root_all.at[1, ym, x, core], root_all.at[1, yp, x, core])),
    ):
        arrived(near[0], p1_s.at[part, 0], p1_r.at[part, 0], plus)
        ahead = near[0].at[pl.ds(0, half)]
        push(ahead, ahead, p1_s.at[part, 2], p1_r.at[part, 2], plus)
        arrived(near[1], p1_s.at[part, 1], p1_r.at[part, 1], minus)
        back = near[1].at[pl.ds(half, half)]
        push(back, back, p1_s.at[part, 3], p1_r.at[part, 3], minus)
    loads[0].wait()
    for part, plus, minus, far in (
        (0, east, west, root_all.at[0, y, x2, core]),
        (1, north, south, root_all.at[1, y2, x, core]),
    ):
        arrived(far.at[pl.ds(0, half)], p1_s.at[part, 2], p1_r.at[part, 2], plus)
        arrived(far.at[pl.ds(half, half)], p1_s.at[part, 3], p1_r.at[part, 3], minus)

    def lines(wave, other):
        cols = pl.ds(wave * T, T)
        real = lambda yy, xs=slice(None): root_all.at[0, yy, xs, other, :, cols]
        imag = lambda xx, ys=slice(None): root_all.at[1, ys, xx, other, :, cols]
        return real, imag

    low, up = pl.ds(0, 2), pl.ds(2, 2)

    def send_near(wave):
        real, imag = lines(wave, core)
        for number, piece, to in (
            (0, real(y), north), (1, real(y), south), (4, imag(x), east), (5, imag(x), west)
        ):
            push(piece, piece, p2_s.at[wave, number], p2_r.at[wave, number], to)

    def to_mate(wave, number, piece):
        push(piece, piece, sib_s.at[wave, number], sib_r.at[wave, number], mate)

    def relay_near(wave):
        real, imag = lines(wave, core)
        for number, piece, ahead, to in (
            (0, real(ym), real(ym, low), north), (1, real(yp), real(yp, up), south),
            (4, imag(xm), imag(xm, low), east), (5, imag(xp), imag(xp, up), west),
        ):
            arrived(piece, p2_s.at[wave, number], p2_r.at[wave, number], to)
            push(ahead, ahead, p2_s.at[wave, number + 2], p2_r.at[wave, number + 2], to)
        to_mate(wave, 0, real(ym))
        to_mate(wave, 1, real(yp))
        to_mate(wave, 2, imag(xm))
        to_mate(wave, 3, imag(xp))

    def relay_far(wave):
        real, imag = lines(wave, core)
        for number, piece, to in (
            (2, real(y2, low), north), (3, real(y2, up), south),
            (6, imag(x2, low), east), (7, imag(x2, up), west),
        ):
            arrived(piece, p2_s.at[wave, number], p2_r.at[wave, number], to)
        to_mate(wave, 4, real(y2))
        to_mate(wave, 5, imag(x2))

    def from_mate(wave):
        real, imag = lines(wave, 1 - core)
        for number, piece in enumerate(
            (real(ym), real(yp), imag(xm), imag(xp), real(y2), imag(x2))
        ):
            arrived(piece, sib_s.at[wave, number], sib_r.at[wave, number], mate)

    send_near(3)
    send_near(2)
    own_line = (root_all.at[0, y, :, core], root_all.at[1, :, x, core])
    for part in range(2):
        push(own_line[part], own_line[part], sib_s.at[NR, part], sib_r.at[NR, part], mate)

    wr = w_ref[0, 0]
    wi = w_ref[0, 1]
    eye = (
        lax.broadcasted_iota(jnp.int32, (T, T), 0) == lax.broadcasted_iota(jnp.int32, (T, T), 1)
    ).astype(F32)

    def weighted_diagonal(real, imag):
        return jnp.sum(fold_rows((wr * real - wi * imag) * eye), axis=0, keepdims=True)

    first, second = pl.ds(0, T), pl.ds(T, T)

    def leaf_inverse(leaf):
        pr, pi = lf[leaf, 0, second, second], lf[leaf, 1, second, second]
        inner = product(
            as_left(*split(pr), *split(pi)),
            as_right(*split(lf[leaf, 0, second, first]), *split(lf[leaf, 1, second, first])),
        )
        ur, ui = lf[leaf, 0, first, second].T, lf[leaf, 1, first, second].T
        tr, ti = inner[:T], inner[T:]
        total = ur * (wr * tr - wi * ti) - ui * (wr * ti + wi * tr)
        base = weighted_diagonal(lf[leaf, 0, first, first], lf[leaf, 1, first, first])
        rows = lax.broadcasted_iota(jnp.int32, (8, T), 0) == 0
        leaf_acc[leaf, 0] = fold_rows(total) + jnp.where(rows, base, 0.0)
        leaf_acc[leaf, 1] = jnp.where(rows, weighted_diagonal(pr, pi), 0.0)

    def turn_upper(leaf):
        for part in range(2):
            for row in (first, second):
                for col in (first, second):
                    lut[leaf, part, col, row] = lu[leaf, part, row, col].T

    def split_lower(leaf):
        for part in range(2):
            for row in (first, second):
                lh[leaf, part, row], lo[leaf, part, row] = split(ll[leaf, part, row])

    def leaf_loop(body):
        def step(leaf, carry):
            body(leaf)
            return carry
        lax.fori_loop(0, 2, step, 0)

    loads[1].wait()
    leaf_loop(leaf_inverse)

    def load_wave(wave):
        for part in range(2):
            def step(row, carry):
                tile = root_all[part, row, :, :, :, pl.ds(wave * T, T)].reshape(T, T)
                fh[part, row, wave], fl[part, row, wave] = split(tile)
                return carry
            lax.fori_loop(0, NR, step, 0)

    def tile_of(high, lower, row, col):
        return high[0, row, col], lower[0, row, col], high[1, row, col], lower[1, row, col]

    def chain(lefts, rights):
        left = jnp.concatenate([as_left(*item) for item in lefts], 1)
        right = jnp.concatenate([as_right(*item) for item in rights], 0)
        return product(left, right)

    def put(row, col, value):
        gh[0, row, col], gl[0, row, col] = split(value[:T])
        gh[1, row, col], gl[1, row, col] = split(value[T:])

    def upper(k, col):
        after = range(k + 1, NR)
        put(k, col, -chain([tile_of(fh, fl, k, m) for m in after], [tile_of(gh, gl, m, col) for m in after]))

    def lower(row, k):
        after = range(k + 1, NR)
        put(row, k, -chain([tile_of(gh, gl, row, m) for m in after], [tile_of(fh, fl, m, k) for m in after]))

    def pivot(k):
        cols = pl.ds(k * T, T)
        real = root_all[0, k, :, :, :, cols].reshape(T, T)
        imag = root_all[1, k, :, :, :, cols].reshape(T, T)
        after = range(k + 1, NR)
        if after:
            taken = chain([tile_of(fh, fl, k, m) for m in after], [tile_of(gh, gl, m, k) for m in after])
            real = real - taken[:T]
            imag = imag - taken[T:]
        gh[0, k, k], gl[0, k, k] = split(real)
        gh[1, k, k], gl[1, k, k] = split(imag)
        small[z, 4 + k : 5 + k] = weighted_diagonal(real, imag)

    relay_near(3)
    send_near(1)
    loads[3].wait()
    leaf_loop(split_lower)
    relay_far(3)
    loads[2].wait()
    leaf_loop(turn_upper)
    relay_near(2)
    send_near(0)
    for part in range(2):
        theirs = (root_all.at[0, y, :, 1 - core], root_all.at[1, :, x, 1 - core])[part]
        arrived(theirs, sib_s.at[NR, part], sib_r.at[NR, part], mate)
    from_mate(3)
    load_wave(3)
    pivot(3)
    upper(2, 3)
    relay_far(2)
    from_mate(2)
    relay_near(1)
    load_wave(2)
    lower(3, 2)
    pivot(2)
    upper(1, 3)
    upper(1, 2)
    relay_far(1)
    relay_near(0)
    from_mate(1)
    load_wave(1)
    lower(3, 1)
    lower(2, 1)
    pivot(1)
    relay_far(0)
    upper(0, 3)
    upper(0, 2)
    upper(0, 1)
    from_mate(0)
    load_wave(0)
    lower(3, 0)
    lower(2, 0)
    lower(1, 0)
    pivot(0)

    def quarter(leaf, number):
        qr, qc = number // 2, number % 2
        cols = pl.ds(pl.multiple_of(qc * T, T), T)
        row = faces_ref[leaf, qr]
        lefts, rights = [], []
        for face in range(2):
            col = faces_ref[leaf, face]
            lefts.append(tile_of(gh, gl, row, col))
            inner = pl.ds(face * T, T)
            rights.append((lh[leaf, 0, inner, cols], lo[leaf, 0, inner, cols],
                           lh[leaf, 1, inner, cols], lo[leaf, 1, inner, cols]))
        block = -chain(lefts, rights)
        real, imag = block[:T], block[T:]
        dr = wr * real - wi * imag
        di = wr * imag + wi * real
        contrib[leaf, number] = dr.reshape(2, 2, sub, T)
        rows = pl.ds(pl.multiple_of(qr * T, T), T)
        taken = lut[leaf, 0, rows, cols] * dr - lut[leaf, 1, rows, cols] * di
        leaf_acc[leaf, qc] = leaf_acc[leaf, qc] - fold_rows(taken)

    def quarters(step):
        def body(leaf, carry):
            number = (z // 2 + (2 * leaf - 1) * step + 8) % 4
            quarter(leaf, number)
            return carry
        lax.fori_loop(0, 2, body, 0)

    def chunk(way, step):
        return (z - step + 16) % Z if way == 0 else (z + step) % Z

    onward = (above, below)

    def mine(way, step, piece):
        number = chunk(way, step)
        return contrib.at[way, number // 2, number % 2, piece]

    def place(way, step, piece):
        number = chunk(way, step)
        block, part = number // 2, number % 2
        row = pl.multiple_of((block // 2) * T + part * (2 * sub) + piece * sub, sub)
        col = pl.multiple_of((block % 2) * T, T)
        return face_out.at[way, pl.ds(row, sub), pl.ds(col, T)]

    def scatter_send(way, step, piece):
        src = mine(way, 0, piece) if step == 0 else rs_buf.at[way, step - 1, piece]
        push(src, rs_buf.at[way, step, piece], rs_s.at[way, step, piece],
             rs_r.at[way, step, piece], onward[way])

    def gather_send(way, step, piece):
        where = place(way, 7 + step, piece)
        push(where, where, ag_s.at[way, step, piece], ag_r.at[way, step, piece], onward[way])

    ways = [(way, piece) for piece in range(2) for way in range(2)]
    quarters(0)
    for way, piece in ways:
        scatter_send(way, 0, piece)
    quarters(1)
    for step in range(Z - 1):
        for way, piece in ways:
            slot = rs_buf.at[way, step, piece]
            arrived(slot, rs_s.at[way, step, piece], rs_r.at[way, step, piece], onward[way])
            if step < Z - 2:
                slot[...] = slot[...] + mine(way, step + 1, piece)[...]
                scatter_send(way, step + 1, piece)
            else:
                place(way, step + 1, piece)[...] = slot[...] + mine(way, step + 1, piece)[...]
                gather_send(way, 0, piece)
        if step < 2:
            quarters(step + 2)
    for leaf in range(2):
        for col in range(2):
            row = 2 * leaf + col
            small[z, row : row + 1] = jnp.sum(leaf_acc[leaf, col], axis=0, keepdims=True)

    def small_send(step):
        where = small.at[(z - step + Z) % Z]
        push(where, where, sm_s.at[step], sm_r.at[step], above)

    small_send(0)
    for step in range(Z - 1):
        arrived(small.at[(z - step - 1 + Z) % Z], sm_s.at[step], sm_r.at[step], above)
        if step < Z - 2:
            small_send(step + 1)
        for way, piece in ways:
            arrived(place(way, 8 + step, piece), ag_s.at[way, step, piece],
                    ag_r.at[way, step, piece], onward[way])
            if step < Z - 2:
                gather_send(way, step + 1, piece)
    total = jnp.sum(small[...], axis=0)
    for leaf in range(2):
        for col in range(2):
            row = 2 * leaf + col
            leaf_out[leaf : leaf + 1, col * T : (col + 1) * T] = total[row : row + 1]
    root_row = jnp.zeros((1, T), F32)
    for k in range(NR):
        root_row = root_row + jnp.where(y == k, total[4 + k : 5 + k], 0.0)
    root_row = pltpu.roll(root_row, (T - (x * 2 + core) * band) % T, 1)
    root_out[...] = root_row[:, :128]
    for copy in sent:
        copy.wait_send()


def per_device(pole_weight, root_factor, leaf_factor, leaf_upper, leaf_lower, face_tiles):
    T = root_factor.shape[-1] // NR
    band = root_factor.shape[2]
    wide = 2 * T
    whole = pl.BlockSpec(memory_space=pl.ANY)
    scalars = pl.BlockSpec(memory_space=pltpu.SMEM)
    vmem = pl.BlockSpec(memory_space=pltpu.VMEM)
    dma = pltpu.SemaphoreType.DMA
    face, leaf, root = pl.pallas_call(
        functools.partial(kernel, T),
        out_shape=(
            jax.ShapeDtypeStruct((2, wide, wide), F32),
            jax.ShapeDtypeStruct((2, wide), F32),
            jax.ShapeDtypeStruct((1, 128), F32),
        ),
        in_specs=[scalars, scalars, whole, whole, whole, whole],
        out_specs=(vmem, vmem, vmem),
        scratch_shapes=[
            pltpu.VMEM((2, Y, X, 2, band, NR * T), F32),
            pltpu.VMEM((2, NR, NR, T, T), BF16),
            pltpu.VMEM((2, NR, NR, T, T), BF16),
            pltpu.VMEM((2, NR, NR, T, T), BF16),
            pltpu.VMEM((2, NR, NR, T, T), BF16),
            pltpu.VMEM((2, 2, wide, wide), F32),
            pltpu.VMEM((2, 2, wide, wide), F32),
            pltpu.VMEM((2, 2, wide, wide), F32),
            pltpu.VMEM((2, 2, wide, wide), F32),
            pltpu.VMEM((2, 2, wide, wide), BF16),
            pltpu.VMEM((2, 2, wide, wide), BF16),
            pltpu.VMEM((2, 4, 2, 2, T // 4, T), F32),
            pltpu.VMEM((2, Z - 1, 2, T // 4, T), F32),
            pltpu.VMEM((2, 2, 8, T), F32),
            pltpu.VMEM((Z, 8, T), F32),
            dma((4,)),
            dma((2, 4)), dma((2, 4)),
            dma((NR, 8)), dma((NR, 8)),
            dma((NR + 1, 6)), dma((NR + 1, 6)),
            dma((2, Z - 1, 2)), dma((2, Z - 1, 2)),
            dma((2, Z - 1, 2)), dma((2, Z - 1, 2)),
            dma((Z - 1,)), dma((Z - 1,)),
        ],
        compiler_params=pltpu.CompilerParams(
            collective_id=0, has_side_effects=True, vmem_limit_bytes=60 * 1024 * 1024
        ),
    )(pole_weight, face_tiles, root_factor[0], leaf_factor[0], leaf_upper[0], leaf_lower[0])
    return root[0, :band], leaf, face


def solution(mesh):
    return jax.shard_map(
        per_device,
        mesh=mesh,
        in_specs=(
            P("pole", None),
            P("pole", None, "snode", None),
            P("pole", "snode", None, None, None),
            P("pole", "snode", None, None, None),
            P("pole", "snode", None, None, None),
            P("snode", None),
        ),
        out_specs=(P("snode"), P("snode", None), P("snode", None, None)),
        check_vma=False,
    )
```

profile of v0, /device:TPU:2, one launch (start us, length us, event | category | flops | bytes accessed | tf_op | source)
XLA Modules:
  0.0 125.0 jit_solution(15427103860464091823)
XLA Ops:
  0.6 118.9 %shard_map.85 = (f32[2,512,512]{2,1,0:T(8,128)}, f32[2,512]{1,0:T(2,128)}, f32[1,128]{1,0:T(1,128)}) custom-call(f32[1,2]{1,0:T(1,128)} %w_ref.1, s32[2,2]{1,0:T(2,128)} %faces_ref.1, f32[2,32,1024]{2,1,0:T(8,128)} %bitcast.9, f32[2,2,512,512]{3,2,1,0:T(8,128)} %bitcast.6, f32[2,2,512,512]{3,2,1,0:T(8,128)} %bitcast.7, f32[2,2,512,512]{3,2,1,0:T(8,128)} %bitcast.8), custom_call_target="tpu_custom_call" | custom-call | tf_op jit(solution)/shard_map/pallas_call | solution.py:414
  119.5 1.1 slice_bitcast_fusion
  120.6 1.3 %copy.11 = f32[2,512]{1,0:T(2,128)} copy(f32[2,512]{1,0:T(2,128)} %get-tuple-element.13) | data formatting | bytes 8192
  121.9 3.1 %copy.12 = f32[2,512,512]{2,1,0:T(8,128)} copy(f32[2,512,512]{2,1,0:T(8,128)} %get-tuple-element.14) | data formatting | bytes 4194304
where the time goes:
time: 125 us
  Pallas kernels  119 us (95%)
  local copies, waits for them, and re-layouts  5.46 us (4%)
    pallas_call x1, Pallas kernels, per_device(): pl.pallas_call(functools.partial(kernel, T), out_shape=(jax.ShapeDtypeStr...  119 us
    unnamed x2, local copies, waits for them, and re-layouts  4.34 us

commit v1 on v0

v1 whole, which is shorter than its diff:
```python
import functools

import jax
import jax.numpy as jnp
from jax import lax
from jax.experimental import pallas as pl
from jax.experimental.pallas import tpu as pltpu
from jax.sharding import PartitionSpec as P

NR = 4
X = 4
Y = 4
Z = 8
HOPS = Z // 2
PIECES = 2
F32 = jnp.float32
BF16 = jnp.bfloat16


def split(value):
    high = value.astype(BF16)
    return high, (value - high.astype(F32)).astype(BF16)


def product(left, right):
    def three(a, b):
        ah, al = (jnp.concatenate([item[n] for item in left], 1) for n in (a, a + 1))
        bh, bl = (jnp.concatenate([item[n] for item in right], 0) for n in (b, b + 1))
        return jnp.dot(
            jnp.concatenate([ah, ah, al], 1), jnp.concatenate([bh, bl, bh], 0), preferred_element_type=F32
        )

    return jnp.concatenate([three(0, 0) - three(2, 2), three(0, 2) + three(2, 0)], 0)


def fold_rows(value):
    rows, cols = value.shape
    return jnp.sum(value.reshape(rows // 8, 8, cols), axis=0)


def kernel(
    T,
    w_ref, faces_ref, root_hbm, lf_hbm, lu_hbm, ll_hbm,
    face_out, leaf_out, root_out,
    root_all, fh, fl, gh, gl, lf, lu, lut, ll, lh, lo, pivots, contrib, rs_buf, leaf_acc, small,
    in_sem, p1_s, p1_r, p2_s, p2_r, sib_s, sib_r, rs_s, rs_r, ag_s, ag_r, sm_s, sm_r,
):
    z = lax.axis_index("pole")
    s = lax.axis_index("snode")
    core = s % 2
    x = (s // 2) % X
    y = s // (2 * X)
    band = root_hbm.shape[1]
    half = band // 2
    sub = T // 2 // PIECES

    def at_xy(yy, xx, cc):
        return {"snode": (yy * X + xx) * 2 + cc}

    xp, xm, x2 = (x + 1) % X, (x + X - 1) % X, (x + 2) % X
    yp, ym, y2 = (y + 1) % Y, (y + Y - 1) % Y, (y + 2) % Y
    zp, zm = (z + 1) % Z, (z + Z - 1) % Z
    east, west = at_xy(y, xp, core), at_xy(y, xm, core)
    north, south = at_xy(yp, x, core), at_xy(ym, x, core)
    mate = at_xy(y, x, 1 - core)
    above, below = {"pole": zp}, {"pole": zm}

    def remote(src, dst, send, recv, to):
        return pltpu.make_async_remote_copy(
            src_ref=src, dst_ref=dst, send_sem=send, recv_sem=recv,
            device_id=to, device_id_type=pl.DeviceIdType.MESH,
        )

    sent = []

    def push(src, dst, send, recv, to):
        copy = remote(src, dst, send, recv, to)
        copy.start()
        sent.append(copy)

    def arrived(dst, send, recv, to):
        remote(dst, dst, send, recv, to).wait_recv()

    barrier = pltpu.get_barrier_semaphore()
    for to in (east, west, north, south, mate, above, below):
        pl.semaphore_signal(barrier, inc=1, device_id=to, device_id_type=pl.DeviceIdType.MESH)

    loads = [
        pltpu.make_async_copy(root_hbm, root_all.at[:, y, x, core], in_sem.at[0]),
        pltpu.make_async_copy(lf_hbm, lf, in_sem.at[1]),
        pltpu.make_async_copy(lu_hbm, lu, in_sem.at[2]),
        pltpu.make_async_copy(ll_hbm, ll, in_sem.at[3]),
    ]
    loads[0].start()
    pl.semaphore_wait(barrier, 7)

    everything = slice(None)
    fore, rear = pl.ds(0, half), pl.ds(half, half)
    halves = (pl.ds(2 * T, 2 * T), pl.ds(0, 2 * T))
    tiles = [pl.ds(wave * T, T) for wave in range(NR)]
    along = ((y, ym, yp, y2), (x, xm, xp, x2))
    across = ((x, xm, xp, x2), (y, ym, yp, y2))
    first_ways = ((east, west), (north, south))
    second_ways = ((north, south), (east, west))

    def spot(part, line, cross, rows, cols, other=core):
        if part == 0:
            return root_all.at[0, line, cross, other, rows, cols]
        return root_all.at[1, cross, line, other, rows, cols]

    def line_send(part, h):
        for number, to in enumerate(first_ways[part]):
            push(root_hbm.at[part, :, halves[h]], spot(part, along[part][0], across[part][0], everything, halves[h]),
                 p1_s.at[part, h, number], p1_r.at[part, h, number], to)

    def line_near(part, h):
        for number, to in enumerate(first_ways[part]):
            cross = across[part][1 + number]
            arrived(spot(part, along[part][0], cross, everything, halves[h]),
                    p1_s.at[part, h, number], p1_r.at[part, h, number], to)
            piece = spot(part, along[part][0], cross, (fore, rear)[number], halves[h])
            push(piece, piece, p1_s.at[part, h, 2 + number], p1_r.at[part, h, 2 + number], to)

    def line_far(part, h):
        for number, to in enumerate(first_ways[part]):
            arrived(spot(part, along[part][0], across[part][3], (fore, rear)[number], halves[h]),
                    p1_s.at[part, h, 2 + number], p1_r.at[part, h, 2 + number], to)

    def near_send(part, group, cut):
        cols = (halves if group == 0 else tiles)[cut]
        for number, to in enumerate(second_ways[part]):
            piece = spot(part, along[part][0], across[part][group], everything, cols)
            src = root_hbm.at[part, :, cols] if group == 0 else piece
            push(src, piece, p2_s.at[part, group, cut, number], p2_r.at[part, group, cut, number], to)

    def far_rows(group, number):
        if group in (0, 3):
            return (fore, rear)[number]
        return everything if group == 1 + number else None

    def near_in(part, group, cut):
        cols = (halves if group == 0 else tiles)[cut]
        for number, to in enumerate(second_ways[part]):
            line = along[part][1 + number]
            arrived(spot(part, line, across[part][group], everything, cols),
                    p2_s.at[part, group, cut, number], p2_r.at[part, group, cut, number], to)
            rows = far_rows(group, number)
            if rows is not None:
                piece = spot(part, line, across[part][group], rows, cols)
                push(piece, piece, p2_s.at[part, group, cut, 2 + number],
                     p2_r.at[part, group, cut, 2 + number], to)

    def far_in(part, group, cut):
        cols = (halves if group == 0 else tiles)[cut]
        for number, to in enumerate(second_ways[part]):
            rows = far_rows(group, number)
            if rows is not None:
                arrived(spot(part, along[part][3], across[part][group], rows, cols),
                        p2_s.at[part, group, cut, 2 + number], p2_r.at[part, group, cut, 2 + number], to)

    parts = (0, 1)

    def mate_lines(cut, numbers, cols, other):
        for part in parts:
            for number in numbers:
                yield part, number, spot(part, along[part][number], everything, everything, cols, other)

    def to_mate(cut, numbers, cols):
        for part, number, piece in mate_lines(cut, numbers, cols, core):
            push(piece, piece, sib_s.at[part, number, cut], sib_r.at[part, number, cut], mate)

    def from_mate(cut, numbers, cols):
        for part, number, piece in mate_lines(cut, numbers, cols, 1 - core):
            arrived(piece, sib_s.at[part, number, cut], sib_r.at[part, number, cut], mate)

    def relay_near(wave):
        for group in (1, 2, 3):
            for part in parts:
                near_in(part, group, wave)
        to_mate(wave, (1, 2), tiles[wave])

    def relay_far(wave):
        for group in (1, 2, 3):
            for part in parts:
                far_in(part, group, wave)
        to_mate(wave, (3,), tiles[wave])

    def waves_send(wave, groups):
        for group in groups:
            for part in parts:
                near_send(part, group, wave)

    def own_part(action, h):
        for part in parts:
            action(part, 0, h)

    def line_part(action, h):
        for part in parts:
            action(part, h)

    def own_line(h):
        to_mate(h, (0,), halves[h])

    def mate_line(h):
        from_mate(h, (0,), halves[h])

    line_part(line_send, 0)
    own_part(near_send, 0)
    for load in loads[1:]:
        load.start()

    wr = w_ref[0, 0]
    wi = w_ref[0, 1]
    eye = (
        lax.broadcasted_iota(jnp.int32, (T, T), 0) == lax.broadcasted_iota(jnp.int32, (T, T), 1)
    ).astype(F32)

    def weighted_diagonal(real, imag):
        return jnp.sum(fold_rows((wr * real - wi * imag) * eye), axis=0, keepdims=True)

    first, second = pl.ds(0, T), pl.ds(T, T)

    def leaf_inverse(leaf):
        pr, pi = lf[leaf, 0, second, second], lf[leaf, 1, second, second]
        inner = product(
            [split(pr) + split(pi)],
            [split(lf[leaf, 0, second, first]) + split(lf[leaf, 1, second, first])],
        )
        ur, ui = lf[leaf, 0, first, second].T, lf[leaf, 1, first, second].T
        tr, ti = inner[:T], inner[T:]
        total = ur * (wr * tr - wi * ti) - ui * (wr * ti + wi * tr)
        base = weighted_diagonal(lf[leaf, 0, first, first], lf[leaf, 1, first, first])
        rows = lax.broadcasted_iota(jnp.int32, (8, T), 0) == 0
        leaf_acc[leaf, 0] = fold_rows(total) + jnp.where(rows, base, 0.0)
        leaf_acc[leaf, 1] = jnp.where(rows, weighted_diagonal(pr, pi), 0.0)

    def turn_upper(leaf):
        for part in range(2):
            for row in (first, second):
                for col in (first, second):
                    lut[leaf, part, col, row] = lu[leaf, part, row, col].T

    def split_lower(leaf):
        for part in range(2):
            for row in (first, second):
                lh[leaf, part, row], lo[leaf, part, row] = split(ll[leaf, part, row])

    def load_wave(wave):
        for part in range(2):
            for row in range(NR):
                if row != wave:
                    tile = root_all[part, row, :, :, :, pl.ds(wave * T, T)].reshape(T, T)
                    fh[part, row, wave], fl[part, row, wave] = split(tile)

    def tile_of(high, lower, row, col):
        return high[0, row, col], lower[0, row, col], high[1, row, col], lower[1, row, col]

    def put(row, col, value):
        gh[0, row, col], gl[0, row, col] = split(value[:T])
        gh[1, row, col], gl[1, row, col] = split(value[T:])

    def uppers(k, cols):
        after = range(k + 1, NR)
        for col in cols:
            put(k, col, -product([tile_of(fh, fl, k, m) for m in after], [tile_of(gh, gl, m, col) for m in after]))

    def lowers(rows, k):
        after = range(k + 1, NR)
        for row in rows:
            put(row, k, -product([tile_of(gh, gl, row, m) for m in after], [tile_of(fh, fl, m, k) for m in after]))

    def pivot(k):
        cols = pl.ds(k * T, T)
        real = root_all[0, k, :, :, :, cols].reshape(T, T)
        imag = root_all[1, k, :, :, :, cols].reshape(T, T)
        after = range(k + 1, NR)
        if after:
            taken = product([tile_of(fh, fl, k, m) for m in after], [tile_of(gh, gl, m, k) for m in after])
            real = real - taken[:T]
            imag = imag - taken[T:]
        gh[0, k, k], gl[0, k, k] = split(real)
        gh[1, k, k], gl[1, k, k] = split(imag)
        pivots[k, 0] = real
        pivots[k, 1] = imag

    def root_diagonal(k):
        small[z, 4 + k : 5 + k] = weighted_diagonal(pivots[k, 0], pivots[k, 1])

    loads[1].wait()
    leaf_inverse(0)
    line_part(line_near, 0)
    waves_send(3, (1, 2))
    line_part(line_send, 1)
    waves_send(2, (1, 2))
    leaf_inverse(1)
    line_part(line_far, 0)
    waves_send(3, (3,))
    waves_send(2, (3,))
    loads[0].wait()
    own_line(0)
    own_part(near_send, 1)
    own_part(near_in, 0)
    line_part(line_near, 1)
    loads[3].wait()
    split_lower(0)
    relay_near(3)
    split_lower(1)
    line_part(line_far, 1)
    own_line(1)
    waves_send(1, (1, 2, 3))
    loads[2].wait()
    turn_upper(0)
    relay_near(2)
    own_part(far_in, 0)
    relay_far(3)
    own_part(near_in, 1)
    waves_send(0, (1, 2, 3))
    turn_upper(1)
    mate_line(0)
    from_mate(3, (1, 2, 3), tiles[3])
    load_wave(3)
    pivot(3)
    uppers(2, (3,))
    relay_near(1)
    relay_far(2)
    from_mate(2, (1, 2, 3), tiles[2])
    load_wave(2)
    lowers((3,), 2)
    pivot(2)
    relay_near(0)
    own_part(far_in, 1)
    relay_far(1)
    uppers(1, (3, 2))
    mate_line(1)
    from_mate(1, (1, 2, 3), tiles[1])
    load_wave(1)
    lowers((3, 2), 1)
    relay_far(0)
    pivot(1)
    uppers(0, (3, 2, 1))
    from_mate(0, (1, 2, 3), tiles[0])
    load_wave(0)
    lowers((3, 2, 1), 0)
    pivot(0)

    def quarter(leaf, number):
        qr, qc = number // 2, number % 2
        cols = pl.ds(pl.multiple_of(qc * T, T), T)
        row = faces_ref[leaf, qr]
        lefts, rights = [], []
        for face in range(2):
            col = faces_ref[leaf, face]
            lefts.append(tile_of(gh, gl, row, col))
            inner = pl.ds(face * T, T)
            rights.append((lh[leaf, 0, inner, cols], lo[leaf, 0, inner, cols],
                           lh[leaf, 1, inner, cols], lo[leaf, 1, inner, cols]))
        block = -product(lefts, rights)
        real, imag = block[:T], block[T:]
        dr = wr * real - wi * imag
        di = wr * imag + wi * real
        contrib[leaf, number] = dr.reshape(2, PIECES, sub, T)
        rows = pl.ds(pl.multiple_of(qr * T, T), T)
        taken = lut[leaf, 0, rows, cols] * dr - lut[leaf, 1, rows, cols] * di
        leaf_acc[leaf, qc] = leaf_acc[leaf, qc] - fold_rows(taken)

    onward = (above, below)
    turns = (1, -1)
    lean = 2 * (z % 2) - 1

    def quarter_step(leaf, step):
        shift = (0, lean, -lean, 2)[step]
        quarter(leaf, ((z + 4) // 2 + shift + 8) % 4)

    def mine(leaf, number, piece):
        return contrib.at[leaf, number // 2, number % 2, piece]

    def place(leaf, number, piece):
        block, part = number // 2, number % 2
        row = pl.multiple_of((block // 2) * T + part * (T // 2) + piece * sub, sub)
        col = pl.multiple_of((block % 2) * T, T)
        return face_out.at[leaf, pl.ds(row, sub), pl.ds(col, T)]

    def owner(way, step):
        return (z + turns[way] * (HOPS - step) + Z) % Z

    def scatter_send(way, step, leaf, piece, src):
        push(src, rs_buf.at[way, step, leaf, piece], rs_s.at[way, step, leaf, piece],
             rs_r.at[way, step, leaf, piece], onward[way])

    def scatter_wait(way, step, leaf, piece):
        slot = rs_buf.at[way, step, leaf, piece]
        arrived(slot, rs_s.at[way, step, leaf, piece], rs_r.at[way, step, leaf, piece], onward[way])
        return slot

    def scatter_first(way, step, leaf):
        for piece in range(PIECES):
            scatter_send(way, step, leaf, piece, mine(leaf, owner(way, step), piece))

    def scatter_on(step, leaf, piece, way):
        slot = scatter_wait(way, step - 1, leaf, piece)
        slot[...] = slot[...] + mine(leaf, owner(way, step), piece)[...]
        scatter_send(way, step, leaf, piece, slot)

    def gather_send(way, step, leaf, piece):
        where = place(leaf, (z - turns[way] * step + Z) % Z, piece)
        push(where, where, ag_s.at[way, step, leaf, piece], ag_r.at[way, step, leaf, piece], onward[way])

    def gather_on(step, leaf, piece, way):
        where = place(leaf, (z - turns[way] * (step + 1) + Z) % Z, piece)
        arrived(where, ag_s.at[way, step, leaf, piece], ag_r.at[way, step, leaf, piece], onward[way])
        if step + 1 < HOPS - 1 or (step + 1 < HOPS and way == leaf):
            gather_send(way, step + 1, leaf, piece)

    for leaf in range(2):
        quarter_step(leaf, 0)
        scatter_first(leaf, 0, leaf)
    for leaf in range(2):
        quarter_step(leaf, 1)
        scatter_first(1 - leaf, 1, leaf)
    for leaf in range(2):
        for piece in range(PIECES):
            scatter_on(1, leaf, piece, leaf)
    for step in range(2, HOPS):
        for leaf in range(2):
            quarter_step(leaf, step)
            for piece in range(PIECES):
                for way in range(2):
                    scatter_on(step, leaf, piece, way)

    def small_send(step):
        where = small.at[(z - step + Z) % Z]
        push(where, where, sm_s.at[step], sm_r.at[step], above)

    def small_on(step):
        arrived(small.at[(z - step - 1 + Z) % Z], sm_s.at[step], sm_r.at[step], above)
        if step < Z - 2:
            small_send(step + 1)

    for leaf in range(2):
        for col in range(2):
            row = 2 * leaf + col
            small[z, row : row + 1] = jnp.sum(leaf_acc[leaf, col], axis=0, keepdims=True)
    for k in range(NR):
        root_diagonal(k)
    small_send(0)
    for leaf in range(2):
        for piece in range(PIECES):
            up = scatter_wait(0, HOPS - 1, leaf, piece)
            down = scatter_wait(1, HOPS - 1, leaf, piece)
            place(leaf, z, piece)[...] = up[...] + down[...] + mine(leaf, z, piece)[...]
            for way in range(2):
                gather_send(way, 0, leaf, piece)
    for step in range(HOPS):
        for leaf in range(2):
            for piece in range(PIECES):
                for way in range(2):
                    if step < HOPS - 1 or way == leaf:
                        gather_on(step, leaf, piece, way)
            if 2 * step + leaf < Z - 1:
                small_on(2 * step + leaf)
    total = jnp.sum(small[...], axis=0)
    for leaf in range(2):
        for col in range(2):
            row = 2 * leaf + col
            leaf_out[leaf : leaf + 1, col * T : (col + 1) * T] = total[row : row + 1]
    root_row = jnp.zeros((1, T), F32)
    for k in range(NR):
        root_row = root_row + jnp.where(y == k, total[4 + k : 5 + k], 0.0)
    root_row = pltpu.roll(root_row, (T - (x * 2 + core) * band) % T, 1)
    root_out[...] = root_row[:, :128]
    for copy in sent:
        copy.wait_send()


def per_device(pole_weight, root_factor, leaf_factor, leaf_upper, leaf_lower, face_tiles):
    T = root_factor.shape[-1] // NR
    band = root_factor.shape[2]
    wide = 2 * T
    whole = pl.BlockSpec(memory_space=pl.ANY)
    scalars = pl.BlockSpec(memory_space=pltpu.SMEM)
    vmem = pl.BlockSpec(memory_space=pltpu.VMEM)
    dma = pltpu.SemaphoreType.DMA
    face, leaf, root = pl.pallas_call(
        functools.partial(kernel, T),
        out_shape=(
            pltpu.VMEM((2, wide, wide), F32),
            pltpu.VMEM((2, wide), F32),
            pltpu.VMEM((1, 128), F32),
        ),
        in_specs=[scalars, scalars, whole, whole, whole, whole],
        out_specs=(vmem, vmem, vmem),
        scratch_shapes=[
            pltpu.VMEM((2, Y, X, 2, band, NR * T), F32),
            pltpu.VMEM((2, NR, NR, T, T), BF16),
            pltpu.VMEM((2, NR, NR, T, T), BF16),
            pltpu.VMEM((2, NR, NR, T, T), BF16),
            pltpu.VMEM((2, NR, NR, T, T), BF16),
            pltpu.VMEM((2, 2, wide, wide), F32),
            pltpu.VMEM((2, 2, wide, wide), F32),
            pltpu.VMEM((2, 2, wide, wide), F32),
            pltpu.VMEM((2, 2, wide, wide), F32),
            pltpu.VMEM((2, 2, wide, wide), BF16),
            pltpu.VMEM((2, 2, wide, wide), BF16),
            pltpu.VMEM((NR, 2, T, T), F32),
            pltpu.VMEM((2, 4, 2, PIECES, T // 2 // PIECES, T), F32),
            pltpu.VMEM((2, HOPS, 2, PIECES, T // 2 // PIECES, T), F32),
            pltpu.VMEM((2, 2, 8, T), F32),
            pltpu.VMEM((Z, 8, T), F32),
            dma((4,)),
            dma((2, 2, 4)), dma((2, 2, 4)),
            dma((2, 4, NR, 4)), dma((2, 4, NR, 4)),
            dma((2, 4, NR)), dma((2, 4, NR)),
            dma((2, HOPS, 2, PIECES)), dma((2, HOPS, 2, PIECES)),
            dma((2, HOPS, 2, PIECES)), dma((2, HOPS, 2, PIECES)),
            dma((Z - 1,)), dma((Z - 1,)),
        ],
        compiler_params=pltpu.CompilerParams(
            collective_id=0, has_side_effects=True, vmem_limit_bytes=60 * 1024 * 1024
        ),
    )(pole_weight, face_tiles, root_factor[0], leaf_factor[0], leaf_upper[0], leaf_lower[0])
    return root[0, :band], leaf, face


def solution(mesh):
    return jax.shard_map(
        per_device,
        mesh=mesh,
        in_specs=(
            P("pole", None),
            P("pole", None, "snode", None),
            P("pole", "snode", None, None, None),
            P("pole", "snode", None, None, None),
            P("pole", "snode", None, None, None),
            P("snode", None),
        ),
        out_specs=(P("snode"), P("snode", None), P("snode", None, None)),
        check_vma=False,
    )
```

time: 125 us -> 102 us (0.82)
  Pallas kernels: 119 us -> 99.2 us
  local copies, waits for them, and re-layouts: 5.46 us -> 2.42 us
    pallas_call x1, Pallas kernels: 119 us -> 99.2 us  [per_device(): pl.pallas_call(functools.partial(kernel, T), out_shape=(pltpu.VMEM((2, wi...]
    unnamed x2, local copies, waits for them, and re-layouts: 4.34 us -> 1.91 us
where the time goes in v1:
time: 102 us
  Pallas kernels  99.2 us (97%)
  local copies, waits for them, and re-layouts  2.42 us (2%)
    pallas_call x1, Pallas kernels, per_device(): pl.pallas_call(functools.partial(kernel, T), out_shape=(pltpu.VMEM((2, wi...  99.2 us

profile of v1, /device:TPU:2, one launch (start us, length us, event | category | flops | bytes accessed | tf_op | source)
XLA Modules:
  0.0 102.2 jit_solution(11987327559246574623)
XLA Ops:
  0.6 99.2 %shard_map.85 = (f32[2,512,512]{2,1,0:T(8,128)S(1)}, f32[2,512]{1,0:T(2,128)S(1)}, f32[1,128]{1,0:T(1,128)S(1)}) custom-call(f32[1,2]{1,0:T(1,128)} %w_ref.1, s32[2,2]{1,0:T(2,128)} %faces_ref.1, f32[2,32,1024]{2,1,0:T(8,128)} %bitcast.9, f32[2,2,512,512]{3,2,1,0:T(8,128)} %bitcast.6, f32[2,2,512,512]{3,2,1,0:T(8,128)} %bitcast.7, f32[2,2,512,512]{3,2,1,0:T(8,128)} %bitcast.8), custom_call_target="tpu_custom_call" | custom-call | tf_op jit(solution)/shard_map/pallas_call | solution.py:483
  99.8 0.5 slice_bitcast_fusion
  100.3 0.6 copy.11
  100.9 1.3 %copy.12 = f32[2,512,512]{2,1,0:T(8,128)} copy(f32[2,512,512]{2,1,0:T(8,128)S(1)} %get-tuple-element.11) | data formatting | bytes 4194304

commit v2 on v1

--- a/solution.py
+++ b/solution.py
@@ -42,8 +42,8 @@
     T,
     w_ref, faces_ref, root_hbm, lf_hbm, lu_hbm, ll_hbm,
     face_out, leaf_out, root_out,
-    root_all, fh, fl, gh, gl, lf, lu, lut, ll, lh, lo, pivots, contrib, rs_buf, leaf_acc, small,
-    in_sem, p1_s, p1_r, p2_s, p2_r, sib_s, sib_r, rs_s, rs_r, ag_s, ag_r, sm_s, sm_r,
+    root_all, fh, fl, gh, gl, lf, lu, lut, ll, lh, lo, pivots, given, taken, contrib, rs_buf, leaf_acc, small,
+    in_sem, p1_s, p1_r, p2_s, p2_r, sib_s, sib_r, rs_s, rs_r, ag_s, ag_r, sm_s, sm_r, ex_s, ex_r,
 ):
     z = lax.axis_index("pole")
     s = lax.axis_index("snode")
@@ -57,9 +57,10 @@
     def at_xy(yy, xx, cc):
         return {"snode": (yy * X + xx) * 2 + cc}
 
-    xp, xm, x2 = (x + 1) % X, (x + X - 1) % X, (x + 2) % X
-    yp, ym, y2 = (y + 1) % Y, (y + Y - 1) % Y, (y + 2) % Y
-    zp, zm = (z + 1) % Z, (z + Z - 1) % Z
+    turn = 1 - 2 * core
+    xp, xm, x2 = (x + turn + X) % X, (x - turn + X) % X, (x + 2) % X
+    yp, ym, y2 = (y + turn + Y) % Y, (y - turn + Y) % Y, (y + 2) % Y
+    zp, zm = (z + turn + Z) % Z, (z - turn + Z) % Z
     east, west = at_xy(y, xp, core), at_xy(y, xm, core)
     north, south = at_xy(yp, x, core), at_xy(ym, x, core)
     mate = at_xy(y, x, 1 - core)
@@ -77,6 +78,11 @@
         copy = remote(src, dst, send, recv, to)
         copy.start()
         sent.append(copy)
+
+    def drain():
+        for copy in sent:
+            copy.wait_send()
+        sent.clear()
 
     def arrived(dst, send, recv, to):
         remote(dst, dst, send, recv, to).wait_recv()
@@ -211,6 +217,7 @@
 
     wr = w_ref[0, 0]
     wi = w_ref[0, 1]
+    own_col = 3 - core
     eye = (
         lax.broadcasted_iota(jnp.int32, (T, T), 0) == lax.broadcasted_iota(jnp.int32, (T, T), 1)
     ).astype(F32)
@@ -259,10 +266,39 @@
         gh[0, row, col], gl[0, row, col] = split(value[:T])
         gh[1, row, col], gl[1, row, col] = split(value[T:])
 
+    def upper_part(k, after, col):
+        return product([tile_of(fh, fl, k, m) for m in after], [tile_of(gh, gl, m, col) for m in after])
+
     def uppers(k, cols):
-        after = range(k + 1, NR)
         for col in cols:
-            put(k, col, -product([tile_of(fh, fl, k, m) for m in after], [tile_of(gh, gl, m, col) for m in after]))
+            put(k, col, -upper_part(k, range(k + 1, NR), col))
+
+    def hand(number):
+        push(given.at[number], taken.at[number], ex_s.at[number], ex_r.at[number], mate)
+
+    def receive(number, row, col):
+        arrived(taken.at[number], ex_s.at[number], ex_r.at[number], mate)
+        put(row, col, taken[number])
+
+    def own_upper_one():
+        value = -upper_part(1, (2, 3), own_col)
+        put(1, own_col, value)
+        given[0] = value
+        hand(0)
+        given[1] = upper_part(0, (2, 3), own_col)
+
+    def own_upper_zero():
+        value = -(given[1] + upper_part(0, (1,), own_col))
+        put(0, own_col, value)
+        given[1] = value
+        hand(1)
+
+    def own_lower_zero():
+        row, after = 3 - core, (1, 2, 3)
+        value = -product([tile_of(gh, gl, row, m) for m in after], [tile_of(fh, fl, m, 0) for m in after])
+        put(row, 0, value)
+        given[2] = value
+        hand(2)
 
     def lowers(rows, k):
         after = range(k + 1, NR)
@@ -275,9 +311,9 @@
         imag = root_all[1, k, :, :, :, cols].reshape(T, T)
         after = range(k + 1, NR)
         if after:
-            taken = product([tile_of(fh, fl, k, m) for m in after], [tile_of(gh, gl, m, k) for m in after])
-            real = real - taken[:T]
-            imag = imag - taken[T:]
+            lost = product([tile_of(fh, fl, k, m) for m in after], [tile_of(gh, gl, m, k) for m in after])
+            real = real - lost[:T]
+            imag = imag - lost[T:]
         gh[0, k, k], gl[0, k, k] = split(real)
         gh[1, k, k], gl[1, k, k] = split(imag)
         pivots[k, 0] = real
@@ -330,18 +366,23 @@
     relay_near(0)
     own_part(far_in, 1)
     relay_far(1)
-    uppers(1, (3, 2))
+    own_upper_one()
     mate_line(1)
     from_mate(1, (1, 2, 3), tiles[1])
     load_wave(1)
     lowers((3, 2), 1)
     relay_far(0)
     pivot(1)
-    uppers(0, (3, 2, 1))
+    own_upper_zero()
+    uppers(0, (1,))
     from_mate(0, (1, 2, 3), tiles[0])
     load_wave(0)
-    lowers((3, 2, 1), 0)
+    receive(0, 1, 2 + core)
+    own_lower_zero()
+    lowers((1,), 0)
+    receive(2, 2 + core, 0)
     pivot(0)
+    receive(1, 0, 2 + core)
 
     def quarter(leaf, number):
         qr, qc = number // 2, number % 2
@@ -360,11 +401,11 @@
         di = wr * imag + wi * real
         contrib[leaf, number] = dr.reshape(2, PIECES, sub, T)
         rows = pl.ds(pl.multiple_of(qr * T, T), T)
-        taken = lut[leaf, 0, rows, cols] * dr - lut[leaf, 1, rows, cols] * di
-        leaf_acc[leaf, qc] = leaf_acc[leaf, qc] - fold_rows(taken)
+        lost = lut[leaf, 0, rows, cols] * dr - lut[leaf, 1, rows, cols] * di
+        leaf_acc[leaf, qc] = leaf_acc[leaf, qc] - fold_rows(lost)
 
     onward = (above, below)
-    turns = (1, -1)
+    turns = (turn, -turn)
     lean = 2 * (z % 2) - 1
 
     def quarter_step(leaf, step):
@@ -411,12 +452,16 @@
         if step + 1 < HOPS - 1 or (step + 1 < HOPS and way == leaf):
             gather_send(way, step + 1, leaf, piece)
 
+    earlier = sent[:]
+    sent.clear()
     for leaf in range(2):
         quarter_step(leaf, 0)
         scatter_first(leaf, 0, leaf)
     for leaf in range(2):
         quarter_step(leaf, 1)
         scatter_first(1 - leaf, 1, leaf)
+    for copy in earlier:
+        copy.wait_send()
     for leaf in range(2):
         for piece in range(PIECES):
             scatter_on(1, leaf, piece, leaf)
@@ -428,11 +473,11 @@
                     scatter_on(step, leaf, piece, way)
 
     def small_send(step):
-        where = small.at[(z - step + Z) % Z]
+        where = small.at[(z - turn * step + Z) % Z]
         push(where, where, sm_s.at[step], sm_r.at[step], above)
 
     def small_on(step):
-        arrived(small.at[(z - step - 1 + Z) % Z], sm_s.at[step], sm_r.at[step], above)
+        arrived(small.at[(z - turn * (step + 1) + Z) % Z], sm_s.at[step], sm_r.at[step], above)
         if step < Z - 2:
             small_send(step + 1)
 
@@ -450,7 +495,12 @@
             place(leaf, z, piece)[...] = up[...] + down[...] + mine(leaf, z, piece)[...]
             for way in range(2):
                 gather_send(way, 0, leaf, piece)
+    scattered = sent[:]
+    sent.clear()
     for step in range(HOPS):
+        if step == 2:
+            for copy in scattered:
+                copy.wait_send()
         for leaf in range(2):
             for piece in range(PIECES):
                 for way in range(2):
@@ -468,8 +518,7 @@
         root_row = root_row + jnp.where(y == k, total[4 + k : 5 + k], 0.0)
     root_row = pltpu.roll(root_row, (T - (x * 2 + core) * band) % T, 1)
     root_out[...] = root_row[:, :128]
-    for copy in sent:
-        copy.wait_send()
+    drain()
 
 
 def per_device(pole_weight, root_factor, leaf_factor, leaf_upper, leaf_lower, face_tiles):
@@ -502,6 +551,8 @@
             pltpu.VMEM((2, 2, wide, wide), BF16),
             pltpu.VMEM((2, 2, wide, wide), BF16),
             pltpu.VMEM((NR, 2, T, T), F32),
+            pltpu.VMEM((3, 2 * T, T), F32),
+            pltpu.VMEM((3, 2 * T, T), F32),
             pltpu.VMEM((2, 4, 2, PIECES, T // 2 // PIECES, T), F32),
             pltpu.VMEM((2, HOPS, 2, PIECES, T // 2 // PIECES, T), F32),
             pltpu.VMEM((2, 2, 8, T), F32),
@@ -513,6 +564,7 @@
             dma((2, HOPS, 2, PIECES)), dma((2, HOPS, 2, PIECES)),
             dma((2, HOPS, 2, PIECES)), dma((2, HOPS, 2, PIECES)),
             dma((Z - 1,)), dma((Z - 1,)),
+            dma((3,)), dma((3,)),
         ],
         compiler_params=pltpu.CompilerParams(
             collective_id=0, has_side_effects=True, vmem_limit_bytes=60 * 1024 * 1024

time: 102 us -> 100 us (0.980)
  Pallas kernels: 99.2 us -> 97.2 us
    pallas_call x1, Pallas kernels: 99.2 us -> 97.2 us  [per_device(): pl.pallas_call(functools.partial(kernel, T), out_shape=(pltpu.VMEM((2, wi...]
where the time goes in v2:
time: 100 us
  Pallas kernels  97.2 us (97%)
  local copies, waits for them, and re-layouts  2.42 us (2%)
    pallas_call x1, Pallas kernels, per_device(): pl.pallas_call(functools.partial(kernel, T), out_shape=(pltpu.VMEM((2, wi...  97.2 us

profile of v2, /device:TPU:2, one launch (start us, length us, event | category | flops | bytes accessed | tf_op | source)
XLA Modules:
  0.0 100.3 jit_solution(9717296053993597610)
XLA Ops:
  0.6 97.2 %shard_map.85 = (f32[2,512,512]{2,1,0:T(8,128)S(1)}, f32[2,512]{1,0:T(2,128)S(1)}, f32[1,128]{1,0:T(1,128)S(1)}) custom-call(f32[1,2]{1,0:T(1,128)} %w_ref.1, s32[2,2]{1,0:T(2,128)} %faces_ref.1, f32[2,32,1024]{2,1,0:T(8,128)} %bitcast.9, f32[2,2,512,512]{3,2,1,0:T(8,128)} %bitcast.6, f32[2,2,512,512]{3,2,1,0:T(8,128)} %bitcast.7, f32[2,2,512,512]{3,2,1,0:T(8,128)} %bitcast.8), custom_call_target="tpu_custom_call" | custom-call | tf_op jit(solution)/shard_map/pallas_call | solution.py:532
  97.8 0.5 slice_bitcast_fusion
  98.4 0.6 copy.11
  99.0 1.3 %copy.12 = f32[2,512,512]{2,1,0:T(8,128)} copy(f32[2,512,512]{2,1,0:T(8,128)S(1)} %get-tuple-element.11) | data formatting | bytes 4194304

commit v3 on v2

--- a/solution.py
+++ b/solution.py
@@ -42,7 +42,7 @@
     T,
     w_ref, faces_ref, root_hbm, lf_hbm, lu_hbm, ll_hbm,
     face_out, leaf_out, root_out,
-    root_all, fh, fl, gh, gl, lf, lu, lut, ll, lh, lo, pivots, given, taken, contrib, rs_buf, leaf_acc, small,
+    root_all, fh, fl, gh, gl, lf, lu, lut, ll, lh, lo, pivots, given, taken, imags, contrib, rs_buf, leaf_acc, small,
     in_sem, p1_s, p1_r, p2_s, p2_r, sib_s, sib_r, rs_s, rs_r, ag_s, ag_r, sm_s, sm_r, ex_s, ex_r,
 ):
     z = lax.axis_index("pole")
@@ -97,7 +97,8 @@
         pltpu.make_async_copy(lu_hbm, lu, in_sem.at[2]),
         pltpu.make_async_copy(ll_hbm, ll, in_sem.at[3]),
     ]
-    loads[0].start()
+    for load in loads:
+        load.start()
     pl.semaphore_wait(barrier, 7)
 
     everything = slice(None)
@@ -116,7 +117,8 @@
 
     def line_send(part, h):
         for number, to in enumerate(first_ways[part]):
-            push(root_hbm.at[part, :, halves[h]], spot(part, along[part][0], across[part][0], everything, halves[h]),
+            push(spot(part, along[part][0], across[part][0], everything, halves[h]),
+                 spot(part, along[part][0], across[part][0], everything, halves[h]),
                  p1_s.at[part, h, number], p1_r.at[part, h, number], to)
 
     def line_near(part, h):
@@ -136,8 +138,7 @@
         cols = (halves if group == 0 else tiles)[cut]
         for number, to in enumerate(second_ways[part]):
             piece = spot(part, along[part][0], across[part][group], everything, cols)
-            src = root_hbm.at[part, :, cols] if group == 0 else piece
-            push(src, piece, p2_s.at[part, group, cut, number], p2_r.at[part, group, cut, number], to)
+            push(piece, piece, p2_s.at[part, group, cut, number], p2_r.at[part, group, cut, number], to)
 
     def far_rows(group, number):
         if group in (0, 3):
@@ -210,20 +211,24 @@
     def mate_line(h):
         from_mate(h, (0,), halves[h])
 
+    loads[0].wait()
     line_part(line_send, 0)
     own_part(near_send, 0)
-    for load in loads[1:]:
-        load.start()
 
     wr = w_ref[0, 0]
     wi = w_ref[0, 1]
     own_col = 3 - core
+    edge = T // 2
     eye = (
-        lax.broadcasted_iota(jnp.int32, (T, T), 0) == lax.broadcasted_iota(jnp.int32, (T, T), 1)
-    ).astype(F32)
+        lax.broadcasted_iota(jnp.int32, (edge, edge), 0) == lax.broadcasted_iota(jnp.int32, (edge, edge), 1)
+    )
 
     def weighted_diagonal(real, imag):
-        return jnp.sum(fold_rows((wr * real - wi * imag) * eye), axis=0, keepdims=True)
+        found = []
+        for begin in (0, edge):
+            block = (slice(begin, begin + edge),) * 2
+            found.append(fold_rows(jnp.where(eye, wr * real[block] - wi * imag[block], 0.0)))
+        return jnp.sum(jnp.concatenate(found, 1), axis=0, keepdims=True)
 
     first, second = pl.ds(0, T), pl.ds(T, T)
 
@@ -332,7 +337,6 @@
     line_part(line_far, 0)
     waves_send(3, (3,))
     waves_send(2, (3,))
-    loads[0].wait()
     own_line(0)
     own_part(near_send, 1)
     own_part(near_in, 0)
@@ -375,14 +379,14 @@
     pivot(1)
     own_upper_zero()
     uppers(0, (1,))
+    receive(0, 1, 2 + core)
+    receive(1, 0, 2 + core)
     from_mate(0, (1, 2, 3), tiles[0])
     load_wave(0)
-    receive(0, 1, 2 + core)
     own_lower_zero()
     lowers((1,), 0)
     receive(2, 2 + core, 0)
     pivot(0)
-    receive(1, 0, 2 + core)
 
     def quarter(leaf, number):
         qr, qc = number // 2, number % 2
@@ -400,8 +404,13 @@
         dr = wr * real - wi * imag
         di = wr * imag + wi * real
         contrib[leaf, number] = dr.reshape(2, PIECES, sub, T)
-        rows = pl.ds(pl.multiple_of(qr * T, T), T)
-        lost = lut[leaf, 0, rows, cols] * dr - lut[leaf, 1, rows, cols] * di
+        imags[leaf, number] = di
+
+    def leaf_diagonal(leaf, number):
+        qr, qc = number // 2, number % 2
+        rows, cols = pl.ds(qr * T, T), pl.ds(qc * T, T)
+        dr = contrib[leaf, number].reshape(T, T)
+        lost = lut[leaf, 0, rows, cols] * dr - lut[leaf, 1, rows, cols] * imags[leaf, number]
         leaf_acc[leaf, qc] = leaf_acc[leaf, qc] - fold_rows(lost)
 
     onward = (above, below)
@@ -482,13 +491,6 @@
             small_send(step + 1)
 
     for leaf in range(2):
-        for col in range(2):
-            row = 2 * leaf + col
-            small[z, row : row + 1] = jnp.sum(leaf_acc[leaf, col], axis=0, keepdims=True)
-    for k in range(NR):
-        root_diagonal(k)
-    small_send(0)
-    for leaf in range(2):
         for piece in range(PIECES):
             up = scatter_wait(0, HOPS - 1, leaf, piece)
             down = scatter_wait(1, HOPS - 1, leaf, piece)
@@ -497,6 +499,16 @@
                 gather_send(way, 0, leaf, piece)
     scattered = sent[:]
     sent.clear()
+    for leaf in range(2):
+        for number in range(4):
+            leaf_diagonal(leaf, number)
+    for leaf in range(2):
+        for col in range(2):
+            row = 2 * leaf + col
+            small[z, row : row + 1] = jnp.sum(leaf_acc[leaf, col], axis=0, keepdims=True)
+    for k in range(NR):
+        root_diagonal(k)
+    small_send(0)
     for step in range(HOPS):
         if step == 2:
             for copy in scattered:
@@ -553,6 +565,7 @@
             pltpu.VMEM((NR, 2, T, T), F32),
             pltpu.VMEM((3, 2 * T, T), F32),
             pltpu.VMEM((3, 2 * T, T), F32),
+            pltpu.VMEM((2, 4, T, T), F32),
             pltpu.VMEM((2, 4, 2, PIECES, T // 2 // PIECES, T), F32),
             pltpu.VMEM((2, HOPS, 2, PIECES, T // 2 // PIECES, T), F32),
             pltpu.VMEM((2, 2, 8, T), F32),

time: 100 us -> 99.9 us (level)
  no operation moved by 1% of the time
where the time goes in v3:
time: 99.9 us; the launch traced here: 99.8 us
  Pallas kernels  96.7 us (97%)
  local copies, waits for them, and re-layouts  2.42 us (2%)
    pallas_call x1, Pallas kernels, per_device(): pl.pallas_call(functools.partial(kernel, T), out_shape=(pltpu.VMEM((2, wi...  96.7 us

profile of v3, /device:TPU:2, one launch (start us, length us, event | category | flops | bytes accessed | tf_op | source)
XLA Modules:
  0.0 99.8 jit_solution(7487530372988432919)
XLA Ops:
  0.6 96.7 %shard_map.85 = (f32[2,512,512]{2,1,0:T(8,128)S(1)}, f32[2,512]{1,0:T(2,128)S(1)}, f32[1,128]{1,0:T(1,128)S(1)}) custom-call(f32[1,2]{1,0:T(1,128)} %w_ref.1, s32[2,2]{1,0:T(2,128)} %faces_ref.1, f32[2,32,1024]{2,1,0:T(8,128)} %bitcast.9, f32[2,2,512,512]{3,2,1,0:T(8,128)} %bitcast.6, f32[2,2,512,512]{3,2,1,0:T(8,128)} %bitcast.7, f32[2,2,512,512]{3,2,1,0:T(8,128)} %bitcast.8), custom_call_target="tpu_custom_call" | custom-call | tf_op jit(solution)/shard_map/pallas_call | solution.py:544
  97.3 0.5 slice_bitcast_fusion
  97.8 0.6 copy.11
  98.4 1.3 %copy.12 = f32[2,512,512]{2,1,0:T(8,128)} copy(f32[2,512,512]{2,1,0:T(8,128)S(1)} %get-tuple-element.11) | data formatting | bytes 4194304

commit v4 on v3

--- a/solution.py
+++ b/solution.py
@@ -42,7 +42,7 @@
     T,
     w_ref, faces_ref, root_hbm, lf_hbm, lu_hbm, ll_hbm,
     face_out, leaf_out, root_out,
-    root_all, fh, fl, gh, gl, lf, lu, lut, ll, lh, lo, pivots, given, taken, imags, contrib, rs_buf, leaf_acc, small,
+    root_all, fh, fl, gh, gl, lf, lu, lut, ll, lh, lo, pivots, given, taken, band_given, band_taken, imags, contrib, rs_buf, leaf_acc, small,
     in_sem, p1_s, p1_r, p2_s, p2_r, sib_s, sib_r, rs_s, rs_r, ag_s, ag_r, sm_s, sm_r, ex_s, ex_r,
 ):
     z = lax.axis_index("pole")
@@ -297,6 +297,24 @@
         put(0, own_col, value)
         given[1] = value
         hand(1)
+
+    def put_band(owner, value):
+        rows = pl.ds(pl.multiple_of(owner * (T // 2), T // 2), T // 2)
+        gh[0, 0, 1, rows], gl[0, 0, 1, rows] = split(value[: T // 2])
+        gh[1, 0, 1, rows], gl[1, 0, 1, rows] = split(value[T // 2 :])
+
+    def own_band_one():
+        after = (1, 2, 3)
+        rows = pl.ds(pl.multiple_of(core * (T // 2), T // 2), T // 2)
+        left = [(fh[0, 0, m, rows], fl[0, 0, m, rows], fh[1, 0, m, rows], fl[1, 0, m, rows]) for m in after]
+        value = -product(left, [tile_of(gh, gl, m, 1) for m in after])
+        put_band(core, value)
+        band_given[...] = value
+        push(band_given, band_taken, ex_s.at[3], ex_r.at[3], mate)
+
+    def receive_band():
+        arrived(band_taken, ex_s.at[3], ex_r.at[3], mate)
+        put_band(1 - core, band_taken[...])
 
     def own_lower_zero():
         row, after = 3 - core, (1, 2, 3)
@@ -378,13 +396,14 @@
     relay_far(0)
     pivot(1)
     own_upper_zero()
-    uppers(0, (1,))
+    own_band_one()
     receive(0, 1, 2 + core)
     receive(1, 0, 2 + core)
     from_mate(0, (1, 2, 3), tiles[0])
     load_wave(0)
     own_lower_zero()
     lowers((1,), 0)
+    receive_band()
     receive(2, 2 + core, 0)
     pivot(0)
 
@@ -565,6 +584,8 @@
             pltpu.VMEM((NR, 2, T, T), F32),
             pltpu.VMEM((3, 2 * T, T), F32),
             pltpu.VMEM((3, 2 * T, T), F32),
+            pltpu.VMEM((T, T), F32),
+            pltpu.VMEM((T, T), F32),
             pltpu.VMEM((2, 4, T, T), F32),
             pltpu.VMEM((2, 4, 2, PIECES, T // 2 // PIECES, T), F32),
             pltpu.VMEM((2, HOPS, 2, PIECES, T // 2 // PIECES, T), F32),
@@ -577,7 +598,7 @@
             dma((2, HOPS, 2, PIECES)), dma((2, HOPS, 2, PIECES)),
             dma((2, HOPS, 2, PIECES)), dma((2, HOPS, 2, PIECES)),
             dma((Z - 1,)), dma((Z - 1,)),
-            dma((3,)), dma((3,)),
+            dma((4,)), dma((4,)),
         ],
         compiler_params=pltpu.CompilerParams(
             collective_id=0, has_side_effects=True, vmem_limit_bytes=60 * 1024 * 1024

time: 99.9 us -> 100 us (level)
  no operation moved by 1% of the time
where the time goes in v4:
time: 100 us; the launch traced here: 99.9 us
  Pallas kernels  96.9 us (97%)
  local copies, waits for them, and re-layouts  2.42 us (2%)
    pallas_call x1, Pallas kernels, per_device(): pl.pallas_call(functools.partial(kernel, T), out_shape=(pltpu.VMEM((2, wi...  96.9 us

profile of v4, /device:TPU:2, one launch (start us, length us, event | category | flops | bytes accessed | tf_op | source)
XLA Modules:
  0.0 99.9 jit_solution(15612979174401845243)
XLA Ops:
  0.6 96.9 %shard_map.85 = (f32[2,512,512]{2,1,0:T(8,128)S(1)}, f32[2,512]{1,0:T(2,128)S(1)}, f32[1,128]{1,0:T(1,128)S(1)}) custom-call(f32[1,2]{1,0:T(1,128)} %w_ref.1, s32[2,2]{1,0:T(2,128)} %faces_ref.1, f32[2,32,1024]{2,1,0:T(8,128)} %bitcast.9, f32[2,2,512,512]{3,2,1,0:T(8,128)} %bitcast.6, f32[2,2,512,512]{3,2,1,0:T(8,128)} %bitcast.7, f32[2,2,512,512]{3,2,1,0:T(8,128)} %bitcast.8), custom_call_target="tpu_custom_call" | custom-call | tf_op jit(solution)/shard_map/pallas_call | solution.py:563
  97.5 0.5 slice_bitcast_fusion
  98.0 0.6 copy.11
  98.6 1.3 %copy.12 = f32[2,512,512]{2,1,0:T(8,128)} copy(f32[2,512,512]{2,1,0:T(8,128)S(1)} %get-tuple-element.11) | data formatting | bytes 4194304
